TPU v7x, 32 devices: a whole 2x2x4 slice. The times are simulated.
32 devices in a mesh: grp: 8 (over y, x, core), mlp: 4 (over z).
Axes of the slice: x: 2, y: 2, z: 4, core: 2. Of those that a mesh axis runs over, the one named last changes fastest.
Arguments:
- queries: bfloat16 [8, 128, 4096], P('grp'), may hold values from -70 to 70
- fresh_kv: bfloat16 [8, 128, 1024], P('grp', 'mlp'), may hold values from -5 to 5
- kv_pages: bfloat16 [8, 32, 128, 1024], P('grp', 'mlp'), may hold values from -5 to 5
- residual: bfloat16 [8, 128, 4096], P('grp'), may hold values from -3 to 3
- norm_gain: float32 [4096], replicated, may hold values from 0.5 to 1.5
- out_weight: bfloat16 [4096, 4096], P('mlp', 'grp'), may hold values from -0.09375 to 0.09375
- gate_weight: bfloat16 [4096, 6144], P('grp', 'mlp'), may hold values from -0.09375 to 0.09375
- up_weight: bfloat16 [4096, 6144], P('grp', 'mlp'), may hold values from -0.09375 to 0.09375
- down_weight: bfloat16 [6144, 4096], P('mlp', 'grp'), may hold values from -0.078125 to 0.078125
- page_table: int32 [8, 16, 12], P('grp'), may hold values from -1 to 31, as said below
- shared_pages: int32 [8, 4], P('grp'), may hold values from 0 to 31, as said below
- cache_lens: int32 [8, 16], P('grp'), may hold values from 513 to 2048, as said below
- prefill_offsets: int32 [8], P('grp'), may hold values from 1 to 512
Outputs:
- layer_out: bfloat16 [8, 128, 4096], P('grp', 'mlp')
Inputs may be any that keep to these rules, and one draw needn't show every extreme that they name: `page_table`: row d lists the pool pages that hold decode d's tokens after the shared prompt, in order, and -1 after its last page; no page appears twice in a group, and none is also a shared page. `shared_pages`: the pool pages of the group's shared prompt in order; they are the first 4 pages of every request of the group. `cache_lens`: decode d's cached tokens fill exactly its listed pages after the 4 shared pages; in every group one decode has the most.
All inputs are finite; a program needn't handle non-finite values.
Results may differ from a plain program's by a relative error of at most 0.029.
Values may be sent and summed in bfloat16 or wider, within the bound.
A program may use at most 128 MiB of HBM per device.

v0:
```python
import jax
import jax.numpy as jnp
from jax import lax
from jax.sharding import PartitionSpec as P

HEADS = 32
KV_HEADS = 4
HEAD = 128
PAGE = 128
SHARED_PAGES = 4
PRIVATE_PAGES = 12
DECODES = 16
PREFILL = 112
ROWS = 128


NEG_FILL = -1e30
EPSILON = 1e-05


def merged(shard, axis, combine):
    everything = jax.tree.map(lambda part: lax.all_gather(part, axis), shard)
    leading = jax.tree.map(lambda part: part[0], everything)

    def step(k, so_far):
        return combine(so_far, jax.tree.map(lambda part: part[k], everything))

    return lax.fori_loop(1, lax.axis_size(axis), step, leading)


def page_layout(page_ids, table_group, shared_group):
    shared_match = shared_group[None, :] == page_ids[:, None]
    is_shared = jnp.any(shared_match, axis=1)
    shared_slot = jnp.sum(
        jnp.where(shared_match, jnp.arange(SHARED_PAGES, dtype=jnp.int32)[None, :], 0),
        axis=1,
        dtype=jnp.int32,
    )
    own_match = table_group[None, :, :] == page_ids[:, None, None]
    owner_id = (
        jnp.sum(
            jnp.where(own_match, jnp.arange(DECODES, dtype=jnp.int32)[None, :, None] + 1, 0),
            axis=(1, 2),
            dtype=jnp.int32,
        )
        - 1
    )
    own_slot = jnp.sum(
        jnp.where(own_match, jnp.arange(PRIVATE_PAGES, dtype=jnp.int32)[None, None, :], 0),
        axis=(1, 2),
        dtype=jnp.int32,
    )
    page_base = jnp.where(is_shared, shared_slot * PAGE, (SHARED_PAGES + own_slot) * PAGE)
    key_pos = (page_base[:, None] + jnp.arange(PAGE, dtype=jnp.int32)[None, :]).reshape(-1)
    key_shared = jnp.repeat(is_shared, PAGE)
    key_owner = jnp.repeat(jnp.where(is_shared, -1, owner_id), PAGE)
    return (key_pos, key_shared, key_owner)


def row_layout(lens_group, offset_value):
    row_ids = jnp.arange(ROWS, dtype=jnp.int32)
    is_prefill = row_ids < PREFILL
    decode_id = jnp.where(is_prefill, -2, row_ids - PREFILL)
    picked = decode_id[:, None] == jnp.arange(DECODES, dtype=jnp.int32)[None, :]
    decode_limit = jnp.sum(jnp.where(picked, lens_group[None, :], 0), axis=1, dtype=jnp.int32)
    limit = jnp.where(is_prefill, offset_value, decode_limit)
    return (row_ids, is_prefill, decode_id, limit)


def cache_visible(key_pos, key_shared, key_owner, decode_id, limit):
    belongs = key_shared[None, :] | (key_owner[None, :] == decode_id[:, None])
    return belongs & (key_pos[None, :] < limit[:, None])


def fresh_visible(key_rows, row_ids, is_prefill):
    before = (key_rows[None, :] < PREFILL) & (key_rows[None, :] <= row_ids[:, None])
    return jnp.where(is_prefill[:, None], before, key_rows[None, :] == row_ids[:, None])


def rms_norm(values, norm_gain):
    return (
        values * lax.rsqrt(jnp.mean(values * values, axis=1, keepdims=True) + EPSILON) * norm_gain
    ).astype(jnp.bfloat16)


def combine_parts(earlier_part, later_part):
    peak_one, total_one, mixed_one = earlier_part
    peak_two, total_two, mixed_two = later_part
    row_peak = jnp.maximum(peak_one, peak_two)
    factor_one = jnp.exp(peak_one - row_peak)
    factor_two = jnp.exp(peak_two - row_peak)
    row_total = total_one * factor_one + total_two * factor_two
    row_number, head_number = row_peak.shape
    weighted = (
        mixed_one.reshape(row_number, head_number, -1) * factor_one[:, :, None]
        + mixed_two.reshape(row_number, head_number, -1) * factor_two[:, :, None]
    )
    return (row_peak, row_total, weighted.reshape(row_number, -1))


def local(
    queries,
    fresh_kv,
    kv_pages,
    residual,
    norm_gain,
    out_weight,
    gate_weight,
    up_weight,
    down_weight,
    page_table,
    shared_pages,
    cache_lens,
    prefill_offsets,
):
    out_rows, gate_cols, up_cols, down_rows = (
        lax.all_gather(out_weight, "grp", axis=1, tiled=True),
        lax.all_gather(gate_weight, "grp", axis=0, tiled=True),
        lax.all_gather(up_weight, "grp", axis=0, tiled=True),
        lax.all_gather(down_weight, "grp", axis=1, tiled=True),
    )
    mlp_index = lax.axis_index("mlp")
    pool_pages = kv_pages.shape[1]
    own_count = fresh_kv.shape[1]
    page_ids = mlp_index * pool_pages + jnp.arange(pool_pages, dtype=jnp.int32)
    key_rows = mlp_index * own_count + jnp.arange(own_count, dtype=jnp.int32)
    key_pos, key_shared, key_owner = page_layout(page_ids, page_table[0], shared_pages[0])
    row_ids, is_prefill, decode_id, limit = row_layout(cache_lens[0], prefill_offsets[0])
    cache_seen = cache_visible(key_pos, key_shared, key_owner, decode_id, limit)
    fresh_seen = fresh_visible(key_rows, row_ids, is_prefill)
    cached = kv_pages[0].reshape(pool_pages * PAGE, 2, KV_HEADS, HEAD)
    fresh = fresh_kv[0].reshape(own_count, 2, KV_HEADS, HEAD)
    grouped = HEADS // KV_HEADS
    query_heads = queries[0].reshape(ROWS, KV_HEADS, grouped, HEAD)
    score_scale = HEAD ** (-0.5)
    peak_list = []
    total_list = []
    mixed_list = []
    for head_index in range(KV_HEADS):
        query_block = query_heads[:, head_index]
        cache_scores = (
            jnp.einsum(
                "rgh,kh->rgk",
                query_block,
                cached[:, 0, head_index],
                preferred_element_type=jnp.float32,
            )
            * score_scale
        )
        fresh_scores = (
            jnp.einsum(
                "rgh,kh->rgk",
                query_block,
                fresh[:, 0, head_index],
                preferred_element_type=jnp.float32,
            )
            * score_scale
        )
        cache_scores = jnp.where(cache_seen[:, None, :], cache_scores, NEG_FILL)
        fresh_scores = jnp.where(fresh_seen[:, None, :], fresh_scores, NEG_FILL)
        row_peak = jnp.maximum(jnp.max(cache_scores, axis=2), jnp.max(fresh_scores, axis=2))
        cache_exps = jnp.where(
            cache_seen[:, None, :], jnp.exp(cache_scores - row_peak[:, :, None]), 0.0
        )
        fresh_exps = jnp.where(
            fresh_seen[:, None, :], jnp.exp(fresh_scores - row_peak[:, :, None]), 0.0
        )
        row_total = jnp.sum(cache_exps, axis=2) + jnp.sum(fresh_exps, axis=2)
        weighted = jnp.einsum(
            "rgk,kh->rgh",
            cache_exps.astype(jnp.bfloat16),
            cached[:, 1, head_index],
            preferred_element_type=jnp.float32,
        )
        weighted = weighted + jnp.einsum(
            "rgk,kh->rgh",
            fresh_exps.astype(jnp.bfloat16),
            fresh[:, 1, head_index],
            preferred_element_type=jnp.float32,
        )
        peak_list.append(row_peak)
        total_list.append(row_total)
        mixed_list.append(weighted)
    row_peak = jnp.stack(peak_list, axis=1).reshape(ROWS, HEADS)
    row_total = jnp.stack(total_list, axis=1).reshape(ROWS, HEADS)
    weighted = jnp.stack(mixed_list, axis=1).reshape(ROWS, HEADS * HEAD)
    row_peak, row_total, weighted = merged((row_peak, row_total, weighted), "mlp", combine_parts)
    attended = (
        (weighted.reshape(ROWS, HEADS, HEAD) / row_total[:, :, None])
        .reshape(ROWS, HEADS * HEAD)
        .astype(jnp.bfloat16)
    )
    feature_count = out_rows.shape[0]
    own_features = lax.dynamic_slice_in_dim(attended, mlp_index * feature_count, feature_count, 1)
    row_begin = mlp_index * own_count
    projected = lax.psum(
        jnp.dot(own_features, out_rows, preferred_element_type=jnp.float32).astype(jnp.bfloat16),
        "mlp",
    ).astype(jnp.float32)
    updated = residual[0].astype(jnp.float32) + projected
    normed = rms_norm(updated, norm_gain)
    carried_rows = lax.dynamic_slice_in_dim(updated, row_begin, own_count, 0)
    gate_act = jnp.dot(normed, gate_cols, preferred_element_type=jnp.float32)
    up_act = jnp.dot(normed, up_cols, preferred_element_type=jnp.float32)
    hidden = (jax.nn.silu(gate_act) * up_act).astype(jnp.bfloat16)
    returned = lax.psum_scatter(
        jnp.dot(hidden, down_rows, preferred_element_type=jnp.float32).astype(jnp.bfloat16),
        "mlp",
        scatter_dimension=0,
        tiled=True,
    ).astype(jnp.float32)
    return (carried_rows + returned).astype(jnp.bfloat16)[None]


def solution(mesh):
    placed = (
        P("grp", None, None),
        P("grp", "mlp", None),
        P("grp", "mlp", None, None),
        P("grp", None, None),
        P(),
        P("mlp", "grp"),
        P("grp", "mlp"),
        P("grp", "mlp"),
        P("mlp", "grp"),
        P("grp", None, None),
        P("grp", None),
        P("grp", None),
        P("grp"),
    )
    return jax.shard_map(
        local, mesh=mesh, in_specs=placed, out_specs=P("grp", "mlp", None), check_vma=False
    )
```

profile of v0, /device:TPU:0, one launch (start us, length us, event | category | flops | bytes accessed | tf_op | source)
XLA Modules:
  0.0 596.7 jit_solution(3144953624618919227)
XLA Ops:
  11.6 3.2 reshape.356
  14.9 4.1 fusion.98
  23.3 3.8 fusion.40
  27.1 2.7 fusion.41
  44.6 3.6 fusion.8
  56.5 6.8 %fusion.10 = (f32[128,8]{0,1:T(8,128)S(1)}, f32[128,8]{0,1:T(8,128)S(1)}, f32[128,8]{0,1:T(8,128)S(1)}) fusion(f32[128,8,1024]{2,0,1:T(8,128)} %copy-done.4, f32[128,8]{0,1:T(8,128)S(1)} %max.80, pred[128,1024]{1,0:T(8,128)(4,1)S(1)} %compare_and_fusion, f32[128,8]{0,1:T(8,128)S(1)} %max.82, f32[128,8,1024]{2,0,1:T(8,128)} %fusion.41, f32[128,8]{0,1:T(8,128)S(1)} %max.84, ...), kind=kLoop, calls=%fused_computation.28 | loop fusion | flops 15725568 | bytes 12738560 | tf_op jit(solution)/shard_map/reduce_sum | solution.py:168
  63.4 20.9 %all_gather.22 = f32[4,128,32]{1,2,0:T(8,128)S(1)} all-gather(f32[1,128,32]{1,2,0:T(8,128)S(1)} %maximum_bitcast_fusion.1), channel_id=1, replica_groups=mesh['grp'=8,'mlp'=4] {'mlp'}, dimensions={0}, use_global_device_ids=true | all-gather | bytes 81920 | tf_op jit(solution)/shard_map/all_gather | solution.py:22
  84.5 14.3 %all_gather.21 = f32[4,128,32]{1,2,0:T(8,128)S(1)} all-gather(f32[1,128,32]{1,2,0:T(8,128)S(1)} %maximum_bitcast_fusion), channel_id=1, replica_groups=mesh['grp'=8,'mlp'=4] {'mlp'}, dimensions={0}, use_global_device_ids=true | all-gather | bytes 81920 | tf_op jit(solution)/shard_map/all_gather | solution.py:22
  98.9 110.8 %all-gather.6.cloned.1.call-done = f32[4,128,4096]{2,1,0:T(8,128)} async-done(((f32[1,128,4096]{2,1,0:T(8,128)}), f32[4,128,4096]{2,1,0:T(8,128)}) %all-gather.6.cloned.1.call-update) | async-done | bytes 8388624 | tf_op jit(solution)/shard_map/all_gather | solution.py:22
  211.4 21.8 %while.19 = (s32[]{:T(128)}, f32[128,32]{1,0:T(8,128)S(1)}, f32[128,32]{1,0:T(8,128)S(1)}, f32[128,4096]{1,0:T(8,128)S(1)}, f32[4,128,32]{1,2,0:T(8,128)S(1)}, /...) while((s32[]{:T(128)}, f32[128,32]{1,0:T(8,128)S(1)}, ...), condition=%wide.region_22.23_spmd, body=%wide.region_21.22_spmd.sunk | while | flops 1597445 | bytes 14975127 | solution.py:28
  212.9 5.7 fusion.111
  220.2 5.8 fusion.111
  227.5 5.7 fusion.111
  233.8 3.0 copy.163
  236.9 29.1 %all-gather.8.cloned.1.call-done = bf16[1024,4096]{1,0:T(8,128)(2,1)} async-done(((bf16[1024,512]{1,0:T(8,128)(2,1)}), bf16[1024,4096]{1,0:T(8,128)(2,1)}) %all-gather.8.cloned.1.call-update) | async-done | bytes 8388624 | tf_op jit(solution)/shard_map/all_gather | solution.py:117
  266.0 5.8 convolution_convert_fusion.1
  273.9 49.9 %all-reduce.2.cloned.1.call-done = bf16[128,4096]{1,0:T(8,128)(2,1)} async-done(((bf16[128,4096]{1,0:T(8,128)(2,1)}), bf16[128,4096]{1,0:T(8,128)(2,1)}) %all-reduce.2.cloned.1.call-update) | async-done | bytes 1048592 | tf_op jit(solution)/shard_map/psum | solution.py:196
  323.8 2.9 convert_add_fusion
  326.8 70.5 %all-gather.10.cloned.1.call-done = bf16[4096,1536]{1,0:T(8,128)(2,1)} async-done(((bf16[512,1536]{1,0:T(8,128)(2,1)}), bf16[4096,1536]{1,0:T(8,128)(2,1)}) %all-gather.10.cloned.1.call-update) | async-done | bytes 12582928 | tf_op jit(solution)/shard_map/all_gather | solution.py:118
  397.2 6.4 %fusion.96 = f32[128,1536]{1,0:T(8,128)S(1)} fusion(bf16[4096,1536]{1,0:T(8,128)(2,1)} %all-gather.10.cloned.1.call-done, f32[4096]{0:T(1024)S(1)} %copy-done.13, f32[128]{0:T(128)S(1)} %add_rsqrt_fusion, bf16[128,4096]{1,0:T(8,128)(2,1)S(1)} %copy-done.3, bf16[1,128,4096]{2,1,0:T(8,128)(2,1)S(1)} %copy-done.2), kind=kOutput, calls=%fused_computation.173 | convolution fusion | flops 1613758464 | bytes 15483392 | tf_op jit(solution)/shard_map/dot_general | solution.py:203
  403.7 67.6 %all-gather.12.cloned.1.call-done = bf16[4096,1536]{1,0:T(8,128)(2,1)} async-done(((bf16[512,1536]{1,0:T(8,128)(2,1)}), bf16[4096,1536]{1,0:T(8,128)(2,1)}) %all-gather.12.cloned.1.call-update) | async-done | bytes 12582928 | tf_op jit(solution)/shard_map/all_gather | solution.py:119
  471.3 76.5 %all-gather.14.cloned.1.call-done = bf16[1536,4096]{1,0:T(8,128)(2,1)} async-done(((bf16[1536,512]{1,0:T(8,128)(2,1)}), bf16[1536,4096]{1,0:T(8,128)(2,1)}) %all-gather.14.cloned.1.call-update) | async-done | bytes 12582928 | tf_op jit(solution)/shard_map/all_gather | solution.py:120
  547.7 12.9 %convolution_convert_fusion = bf16[128,4096]{1,0:T(8,128)(2,1)} fusion(bf16[1536,4096]{1,0:T(8,128)(2,1)} %all-gather.14.cloned.1.call-done, bf16[4096,1536]{1,0:T(8,128)(2,1)} %all-gather.12.cloned.1.call-done, f32[128,1536]{1,0:T(8,128)S(1)} %fusion.96, f32[4096]{0:T(1024)S(1)} %copy-done.13, f32[128]{0:T(128)S(1)} %add_rsqrt_fusion, ...), kind=kOutput, calls=%fused_computation.11 | convolution fusion | flops 3226075136 | bytes 29114880 | tf_op jit(solution)/shard_map/dot_general | solution.py:207
  560.7 27.3 %reduce-scatter.2.cloned.1.call-done = bf16[32,4096]{1,0:T(8,128)(2,1)} async-done(((bf16[128,4096]{1,0:T(8,128)(2,1)}), bf16[32,4096]{1,0:T(8,128)(2,1)}) %reduce-scatter.2.cloned.1.call-update) | async-done | bytes 262160 | tf_op jit(solution)/shard_map/reduce_scatter | solution.py:206
  (134 shorter events, 42.4 us)
Async XLA Ops:
  6.5 203.1 %all-gather.6.cloned.1.call-start = ((), (), s32[]{:S(2)}) async-start(), calls=%async_computation.1 | async-start | bytes 10485760 | tf_op jit(solution)/shard_map/all_gather | solution.py:22
  7.8 3.2 copy-start.21
  14.9 5.8 copy-start.14
  23.3 3.8 copy-start.7
  23.3 7.5 %copy-start.5 = (bf16[1024,1,1,128]{3,2,1,0:T(2,128)(2,1)S(1)}, bf16[1024,1,1,128]{3,2,1,0:T(2,128)(2,1)}, u32[]{:S(2)}) copy-start(bf16[1024,1,1,128]{3,2,1,0:T(2,128)(2,1)} %get-tuple-element.241) | copy-start | bytes 786436
  27.1 12.4 %copy-start.6 = (bf16[1024,1,1,128]{3,2,1,0:T(2,128)(2,1)S(1)}, bf16[1024,1,1,128]{3,2,1,0:T(2,128)(2,1)}, u32[]{:S(2)}) copy-start(bf16[1024,1,1,128]{3,2,1,0:T(2,128)(2,1)} %get-tuple-element.245) | copy-start | bytes 786436
  34.3 6.8 %copy-start.10 = (bf16[1024,1,1,128]{0,3,2,1:T(8,128)(2,1)S(1)}, bf16[1024,1,1,128]{0,3,2,1:T(8,128)(2,1)}, u32[]{:S(2)}) copy-start(bf16[1024,1,1,128]{0,3,2,1:T(8,128)(2,1)} %copy.112) | copy-start | bytes 786436
  39.5 3.0 copy-start.8
  41.1 2.2 copy-start
  41.1 3.5 copy-start.1
  44.6 3.6 copy-start.19
  44.6 3.6 copy-start.11
  48.2 3.1 copy-start.4
  51.3 1.7 copy-start.16
  51.3 1.9 copy-start.15
  55.6 210.4 %all-gather.8.cloned.1.call-start = ((), (), s32[]{:S(2)}) async-start(), calls=%async_computation.2 | async-start | bytes 9437184 | tf_op jit(solution)/shard_map/all_gather | solution.py:117
  56.3 267.5 %all-reduce.2.cloned.1.call-start = ((), (), s32[]{:S(2)}) async-start(), calls=%async_computation.3 | async-start | bytes 2097152 | tf_op jit(solution)/shard_map/psum | solution.py:196
  271.8 52.0 %copy-start.2 = (bf16[1,128,4096]{2,1,0:T(8,128)(2,1)S(1)}, bf16[1,128,4096]{2,1,0:T(8,128)(2,1)}, u32[]{:S(2)}) copy-start(bf16[1,128,4096]{2,1,0:T(8,128)(2,1)} %param.18) | copy-start | bytes 3145732
  271.8 125.4 %copy-start.13 = (f32[4096]{0:T(1024)S(1)}, f32[4096]{0:T(1024)}, u32[]{:S(2)}) copy-start(f32[4096]{0:T(1024)} %param.19) | copy-start | bytes 49156
  271.8 125.4 %all-gather.10.cloned.1.call-start = ((), (), s32[]{:S(2)}) async-start(), calls=%async_computation.4 | async-start | bytes 14155776 | tf_op jit(solution)/shard_map/all_gather | solution.py:118
  272.4 198.9 %all-gather.12.cloned.1.call-start = ((), (), s32[]{:S(2)}) async-start(), calls=%async_computation.5 | async-start | bytes 14155776 | tf_op jit(solution)/shard_map/all_gather | solution.py:119
  273.0 274.8 %all-gather.14.cloned.1.call-start = ((), (), s32[]{:S(2)}) async-start(), calls=%async_computation.6 | async-start | bytes 14155776 | tf_op jit(solution)/shard_map/all_gather | solution.py:120
  273.6 314.4 %reduce-scatter.2.cloned.1.call-start = ((), (), s32[]{:S(2)}) async-start(), calls=%async_computation.7 | async-start | bytes 1310720 | tf_op jit(solution)/shard_map/reduce_scatter | solution.py:206
  323.8 73.5 %copy-start.3 = (bf16[128,4096]{1,0:T(8,128)(2,1)S(1)}, bf16[128,4096]{1,0:T(8,128)(2,1)}, u32[]{:S(2)}) copy-start(bf16[128,4096]{1,0:T(8,128)(2,1)} %all-reduce.2.cloned.1.call-done) | copy-start | bytes 3145732
  (5 other events, 6.6 us)
Sparse Core Ops, SparseCore 0:
  55.7 153.9 all-gather.5
  211.5 54.4 all-gather.7
  271.9 51.8 all-reduce.1
  325.7 71.4 all-gather.9
  399.1 72.1 all-gather.11
  473.2 74.5 all-gather.13
  560.8 27.1 reduce-scatter.1
where the time goes:
time: 597 us
  waiting for transfers between devices  434 us (73%)
  matrix products  46 us (8%)
  other arithmetic  36.5 us (6%)
  blocking collectives  35.3 us (6%)
  local copies, waits for them, and re-layouts  29.8 us (5%)
  between operations  14.6 us (2%)
    all_gather x1, waiting for transfers between devices, merged(): everything = jax.tree.map(lambda part: lax.all_gather(part, axis), shard)  111 us
    all_gather x1, waiting for transfers between devices, local(): lax.all_gather(down_weight, 'grp', axis=1, tiled=True)  76.5 us
    all_gather x1, waiting for transfers between devices, local(): lax.all_gather(gate_weight, 'grp', axis=0, tiled=True)  70.5 us
    all_gather x1, waiting for transfers between devices, local(): lax.all_gather(up_weight, 'grp', axis=0, tiled=True)  67.6 us
    psum x1, waiting for transfers between devices, local(): lax.psum(jnp.dot(own_features, out_rows, preferred_element_type=jnp.float...  49.9 us
    all_gather x2, blocking collectives, merged(): everything = jax.tree.map(lambda part: lax.all_gather(part, axis), shard)  35.3 us
    all_gather x1, waiting for transfers between devices, local(): lax.all_gather(out_weight, 'grp', axis=1, tiled=True)  29.1 us
    reduce_scatter x1, waiting for transfers between devices, local(): lax.psum_scatter(jnp.dot(hidden, down_rows, preferred_element_type=jnp.fl...  27.3 us
  transfers between devices with their start and end apart: 7, of which 7 were waited for; matrix products, arithmetic and copies ran while one was open for 7% of the time, Pallas kernels for 0%

commit v1 on v0

v1 whole, which is shorter than its diff:
```python
import functools

import jax
import jax.numpy as jnp
from jax import lax
from jax.experimental import pallas as pl
from jax.experimental.pallas import tpu as pltpu
from jax.sharding import PartitionSpec as P

HEADS = 32
KV_HEADS = 4
HEAD = 128
PAGE = 128
SHARED_PAGES = 4
PRIVATE_PAGES = 12
DECODES = 16
PREFILL = 112
ROWS = 128
GROUPED = HEADS // KV_HEADS

NEG_FILL = -1e30
EPSILON = 1e-05
MESH = pl.DeviceIdType.MESH
F32 = jnp.float32
BF16 = jnp.bfloat16


def tile_of(width):
    return 256 if width % 256 == 0 else 128


def kernel(
    n,
    chips,
    queries,
    kv_pages,
    fresh_kv,
    gain,
    table,
    shared,
    lens,
    offset,
    residual,
    out_weight,
    gate_weight,
    up_weight,
    down_weight,
    out,
    bias,
    fresh_bias,
    part_send,
    part_recv,
    stat_send,
    stat_recv,
    res,
    out_w,
    gate_w,
    up_w,
    down_w,
    att,
    proj_part,
    proj_recv,
    proj,
    upd,
    normed,
    gu,
    gu_recv,
    ssq,
    ssq_recv,
    hid,
    down_part,
    down_recv,
    fin,
    fin_recv,
    weight_local,
    weight_send,
    weight_recv,
    res_local,
    res_send,
    res_recv,
    part_ss,
    part_rs,
    stat_ss,
    stat_rs,
    att_ss,
    att_rs,
    rs_ss,
    rs_rs,
    ag_ss,
    ag_rs,
    gu_ss,
    gu_rs,
    ssq_ss,
    ssq_rs,
    hid_ss,
    hid_rs,
    down_ss,
    down_rs,
    fin_ss,
    fin_rs,
):
    me = lax.axis_index("mlp")
    grp = lax.axis_index("grp")
    chip = grp // 2
    core = grp % 2
    parts = res.shape[0]
    piece = res.shape[3]
    width = out_w.shape[2]
    cols = 2 * width
    feats = att.shape[-1]
    hidden = hid.shape[-1]
    block_heads = feats // HEAD
    rows = n * chips * piece

    def along(j):
        return {"mlp": lax.rem(me + j, n)}

    def across(j):
        return {"grp": lax.rem(chip + j, chips) * 2 + core}

    def back(j):
        return {"grp": lax.rem(chip + chips - j, chips) * 2 + core}

    partner = {"grp": chip * 2 + (1 - core)}

    def send(src, dst, ss, rs, device):
        copy = pltpu.make_async_remote_copy(
            src_ref=src,
            dst_ref=dst,
            send_sem=ss,
            recv_sem=rs,
            device_id=device,
            device_id_type=MESH,
        )
        copy.start()
        return copy

    barrier = pltpu.get_barrier_semaphore()
    for j in range(1, n):
        pl.semaphore_signal(barrier, inc=1, device_id=along(j), device_id_type=MESH)
    for j in range(1, chips):
        pl.semaphore_signal(barrier, inc=1, device_id=across(j), device_id_type=MESH)
    pl.semaphore_signal(barrier, inc=1, device_id=partner, device_id_type=MESH)

    local_weights = (
        (out_weight, out_w.at[core]),
        (gate_weight, gate_w.at[core]),
        (up_weight, up_w.at[core]),
        (down_weight, down_w.at[core]),
    )
    held = []
    for i, (src, dst) in enumerate(local_weights):
        copy = pltpu.make_async_copy(src, dst, weight_local.at[i])
        copy.start()
        held.append(copy)
    own_res = []
    for q in range(parts):
        copy = pltpu.make_async_copy(
            residual.at[:, q, :, pl.ds(pl.multiple_of(chip * cols, cols), cols)],
            res.at[q, :, 0],
            res_local.at[q],
        )
        copy.start()
        own_res.append(copy)

    pl.semaphore_wait(barrier, n + chips - 1)

    paired = []
    for i, (src, dst) in enumerate(local_weights):
        paired.append(send(src, dst, weight_send.at[i], weight_recv.at[i], partner))
    res_copies = []
    for q in range(parts):
        for j in range(1, chips):
            start = pl.multiple_of(lax.rem(chip + j, chips) * cols, cols)
            res_copies.append(
                send(
                    residual.at[:, q, :, pl.ds(start, cols)],
                    res.at[q, :, j],
                    res_send.at[q, j],
                    res_recv.at[q, j],
                    across(j),
                )
            )

    pool_pages = kv_pages.shape[0] // PAGE
    own_count = fresh_kv.shape[0]
    token = lax.broadcasted_iota(jnp.int32, (1, PAGE), 1)
    slot_ids = lax.broadcasted_iota(jnp.int32, (DECODES, PRIVATE_PAGES), 1)
    shared_ids = lax.broadcasted_iota(jnp.int32, (1, SHARED_PAGES), 1)
    for p in range(pool_pages):
        page_id = me * pool_pages + p
        own = table[...] == page_id
        own_any = jnp.max(jnp.where(own, 1, 0), axis=1, keepdims=True)
        own_base = jnp.sum(
            jnp.where(own, (SHARED_PAGES + slot_ids) * PAGE, 0), axis=1, keepdims=True
        )
        match = shared[...] == page_id
        is_shared = jnp.max(jnp.where(match, 1, 0), axis=1, keepdims=True)
        shared_base = jnp.sum(jnp.where(match, shared_ids * PAGE, 0), axis=1, keepdims=True)
        position = shared_base + token
        seen = (is_shared > 0) & (position < offset[...])
        bias[0:PREFILL, p * PAGE : (p + 1) * PAGE] = jnp.broadcast_to(
            jnp.where(seen, 0.0, NEG_FILL), (PREFILL, PAGE)
        )
        belongs = jnp.maximum(own_any, is_shared)
        base = jnp.where(is_shared > 0, shared_base, own_base)
        seen = (belongs > 0) & (base + token < lens[...])
        bias[PREFILL:ROWS, p * PAGE : (p + 1) * PAGE] = jnp.where(seen, 0.0, NEG_FILL)
    row_ids = lax.broadcasted_iota(jnp.int32, (ROWS, own_count), 0)
    key_rows = me * own_count + lax.broadcasted_iota(jnp.int32, (ROWS, own_count), 1)
    seen = ((row_ids < PREFILL) & (key_rows < PREFILL) & (key_rows <= row_ids)) | (
        (row_ids >= PREFILL) & (key_rows == row_ids)
    )
    fresh_bias[...] = jnp.where(seen, 0.0, NEG_FILL)

    lane = lax.broadcasted_iota(jnp.int32, (ROWS, HEAD), 1)
    scale = HEAD ** (-0.5)
    keys_across = (((1,), (1,)), ((), ()))
    value_at = KV_HEADS * HEAD

    part_copies = []
    stat_copies = []
    for j in range(1, n + 1):
        block = lax.rem(me + j, n)

        def one_head(i, stats, block=block):
            head = block * block_heads + i
            key_start = pl.multiple_of((head // GROUPED) * HEAD, HEAD)
            query = queries[:, pl.ds(pl.multiple_of(head * HEAD, HEAD), HEAD)]
            scores = (
                lax.dot_general(
                    query,
                    kv_pages[:, pl.ds(key_start, HEAD)],
                    keys_across,
                    preferred_element_type=F32,
                )
                * scale
                + bias[...]
            )
            fresh_scores = (
                lax.dot_general(
                    query,
                    fresh_kv[:, pl.ds(key_start, HEAD)],
                    keys_across,
                    preferred_element_type=F32,
                )
                * scale
                + fresh_bias[...]
            )
            peak = jnp.maximum(
                jnp.max(scores, axis=1, keepdims=True),
                jnp.max(fresh_scores, axis=1, keepdims=True),
            )
            exps = jnp.exp(scores - peak)
            fresh_exps = jnp.exp(fresh_scores - peak)
            total = jnp.sum(exps, axis=1, keepdims=True) + jnp.sum(
                fresh_exps, axis=1, keepdims=True
            )
            mixed = jnp.dot(
                exps.astype(BF16),
                kv_pages[:, pl.ds(value_at + key_start, HEAD)],
                preferred_element_type=F32,
            ) + jnp.dot(
                fresh_exps.astype(BF16),
                fresh_kv[:, pl.ds(value_at + key_start, HEAD)],
                preferred_element_type=F32,
            )
            part_send[block, :, pl.ds(pl.multiple_of(i * HEAD, HEAD), HEAD)] = (
                mixed / total
            ).astype(BF16)
            return jnp.where(lane == i, peak + jnp.log(total), stats)

        stats = lax.fori_loop(0, block_heads, one_head, jnp.zeros((ROWS, HEAD), F32), unroll=2)
        stat_send[block] = stats.T[0:8]
        if j < n:
            part_copies.append(
                send(part_send.at[block], part_recv.at[j], part_ss.at[j], part_rs.at[j], along(j))
            )
            stat_copies.append(
                send(stat_send.at[block], stat_recv.at[j], stat_ss.at[j], stat_rs.at[j], along(j))
            )

    for copy in stat_copies + part_copies:
        copy.wait_recv()
    levels = [stat_send[me].T] + [stat_recv[j].T for j in range(1, n)]
    top = functools.reduce(jnp.maximum, levels)
    shares = [jnp.exp(level - top) for level in levels]
    whole = functools.reduce(jnp.add, shares)
    shares = [share / whole for share in shares]
    for i in range(block_heads):
        span = slice(i * HEAD, (i + 1) * HEAD)
        value = part_send[me, :, span].astype(F32) * shares[0][:, i : i + 1]
        for j in range(1, n):
            value = value + part_recv[j, :, span].astype(F32) * shares[j][:, i : i + 1]
        value = value.astype(BF16).reshape(n, parts, piece, HEAD)
        for q in range(parts):
            att[q, :, 0, :, span] = value[:, q]
    att_copies = [[] for _ in range(parts)]
    for q in range(parts):
        for j in range(1, chips):
            att_copies[q].append(
                send(att.at[q, :, 0], att.at[q, :, j], att_ss.at[q, j], att_rs.at[q, j], across(j))
            )

    held[0].wait()
    paired[0].wait_recv()
    rs_copies = [[] for _ in range(parts)]
    tile = tile_of(width)
    for q in range(parts):
        for copy in att_copies[q]:
            copy.wait_recv()
        for half in range(2):

            @pl.loop(0, width // tile)
            def _(t, q=q, half=half):
                at = pl.multiple_of(t * tile, tile)
                value = jnp.dot(
                    att[q].reshape(rows, feats),
                    out_w[half, :, pl.ds(at, tile)],
                    preferred_element_type=F32,
                )
                proj_part[q, :, :, :, pl.ds(pl.multiple_of(half * width + at, tile), tile)] = (
                    value.astype(BF16).reshape(n, chips, piece, tile)
                )

        for j in range(1, n):
            rs_copies[q].append(
                send(
                    proj_part.at[q, lax.rem(me + j, n)],
                    proj_recv.at[q, j],
                    rs_ss.at[q, j],
                    rs_rs.at[q, j],
                    along(j),
                )
            )
    ag_copies = [[] for _ in range(parts)]
    for q in range(parts):
        for copy in rs_copies[q]:
            copy.wait_recv()
        value = proj_part[q, me].astype(F32)
        for j in range(1, n):
            value = value + proj_recv[q, j].astype(F32)
        proj[q, me] = value.astype(BF16)
        for j in range(1, n):
            ag_copies[q].append(
                send(proj.at[q, me], proj.at[q, me], ag_ss.at[q, j], ag_rs.at[q, j], along(j))
            )

    for copy in own_res:
        copy.wait()
    for copy in res_copies:
        copy.wait_recv()
    for i in (1, 2):
        held[i].wait()
        paired[i].wait_recv()
    gain_here = gain[:, pl.ds(pl.multiple_of(chip * cols, cols), cols)]
    gu_copies = [[] for _ in range(parts)]
    tile = tile_of(hidden)
    for q in range(parts):
        for j in range(1, n):
            other = lax.rem(me + n - j, n)
            pltpu.make_async_remote_copy(
                src_ref=proj.at[q, other],
                dst_ref=proj.at[q, other],
                send_sem=ag_ss.at[q, j],
                recv_sem=ag_rs.at[q, j],
                device_id=along(j),
                device_id_type=MESH,
            ).wait_recv()

        @pl.loop(0, n)
        def _(p, q=q):
            value = res[q, p].astype(F32) + proj[q, p].astype(F32)
            upd[q, p] = value
            square = jnp.sum(value * value, axis=2, keepdims=True)
            ssq[q, p] = jnp.broadcast_to(square, (chips, piece, HEAD))
            normed[q, p] = (value * gain_here[None]).astype(BF16)

        for j in range(1, chips):
            gu_copies[q].append(
                send(ssq.at[q, :, j], ssq_recv.at[q, j], ssq_ss.at[q, j], ssq_rs.at[q, j], back(j))
            )
        for which, weight in enumerate((gate_w, up_w)):

            @pl.loop(0, hidden // tile)
            def _(t, q=q, which=which, weight=weight):
                at = pl.multiple_of(t * tile, tile)
                value = jnp.dot(
                    normed[q].reshape(rows, cols),
                    weight[:, :, pl.ds(at, tile)].reshape(cols, tile),
                    preferred_element_type=F32,
                )
                gu[q, which, :, :, :, pl.ds(at, tile)] = value.astype(BF16).reshape(
                    n, chips, piece, tile
                )

            for j in range(1, chips):
                gu_copies[q].append(
                    send(
                        gu.at[q, which, :, j],
                        gu_recv.at[q, j, which],
                        gu_ss.at[q, j, which],
                        gu_rs.at[q, j, which],
                        back(j),
                    )
                )

    hid_copies = [[] for _ in range(parts)]
    for q in range(parts):
        for copy in gu_copies[q]:
            copy.wait_recv()

        @pl.loop(0, n)
        def _(p, q=q):
            square = ssq[q, p, 0]
            for j in range(1, chips):
                square = square + ssq_recv[q, j, p]
            factor = lax.rsqrt(square[:, 0:1] / (chips * cols) + EPSILON)
            gate = gu[q, 0, p, 0].astype(F32)
            up = gu[q, 1, p, 0].astype(F32)
            for j in range(1, chips):
                gate = gate + gu_recv[q, j, 0, p].astype(F32)
                up = up + gu_recv[q, j, 1, p].astype(F32)
            gate = gate * factor
            up = up * factor
            hid[q, p, 0] = (gate / (1.0 + jnp.exp(-gate)) * up).astype(BF16)

        for j in range(1, chips):
            hid_copies[q].append(
                send(hid.at[q, :, 0], hid.at[q, :, j], hid_ss.at[q, j], hid_rs.at[q, j], across(j))
            )

    held[3].wait()
    paired[3].wait_recv()
    down_copies = [[] for _ in range(parts)]
    tile = tile_of(width)
    for q in range(parts):
        for copy in hid_copies[q]:
            copy.wait_recv()
        for half in range(2):

            @pl.loop(0, width // tile)
            def _(t, q=q, half=half):
                at = pl.multiple_of(t * tile, tile)
                value = jnp.dot(
                    hid[q].reshape(rows, hidden),
                    down_w[half, :, pl.ds(at, tile)],
                    preferred_element_type=F32,
                )
                down_part[q, :, :, :, pl.ds(pl.multiple_of(half * width + at, tile), tile)] = (
                    value.astype(BF16).reshape(n, chips, piece, tile)
                )

        for j in range(1, n):
            down_copies[q].append(
                send(
                    down_part.at[q, lax.rem(me + j, n)],
                    down_recv.at[q, j],
                    down_ss.at[q, j],
                    down_rs.at[q, j],
                    along(j),
                )
            )
    fin_copies = [[] for _ in range(parts)]
    for q in range(parts):
        for copy in down_copies[q]:
            copy.wait_recv()
        value = down_part[q, me].astype(F32)
        for j in range(1, n):
            value = value + down_recv[q, j].astype(F32)
        fin[q] = (upd[q, me] + value).astype(BF16)
        for j in range(1, chips):
            fin_copies[q].append(
                send(fin.at[q, j], fin_recv.at[q, j], fin_ss.at[q, j], fin_rs.at[q, j], back(j))
            )
    for q in range(parts):
        out[q, :, pl.ds(pl.multiple_of(chip * cols, cols), cols)] = fin[q, 0]
        for copy in fin_copies[q]:
            copy.wait_recv()
        for j in range(1, chips):
            start = pl.multiple_of(lax.rem(chip + j, chips) * cols, cols)
            out[q, :, pl.ds(start, cols)] = fin_recv[q, j]

    sent = paired + res_copies + part_copies + stat_copies
    for group in (att_copies, rs_copies, ag_copies, gu_copies, hid_copies, down_copies, fin_copies):
        for copies in group:
            sent = sent + copies
    for copy in sent:
        copy.wait_send()


def local(
    n,
    chips,
    queries,
    fresh_kv,
    kv_pages,
    residual,
    norm_gain,
    out_weight,
    gate_weight,
    up_weight,
    down_weight,
    page_table,
    shared_pages,
    cache_lens,
    prefill_offsets,
):
    own = fresh_kv.shape[1]
    parts = max(1, own // 16)
    piece = own // parts
    width = out_weight.shape[1]
    cols = 2 * width
    feats = out_weight.shape[0]
    hidden = gate_weight.shape[1]
    model = norm_gain.shape[0]
    pool = kv_pages.shape[1] * PAGE
    vmem = pl.BlockSpec(memory_space=pltpu.VMEM)
    anywhere = pl.BlockSpec(memory_space=pl.ANY)

    def dma(*shape):
        return [pltpu.SemaphoreType.DMA(shape)] * 2

    result = pl.pallas_call(
        functools.partial(kernel, n, chips),
        out_shape=jax.ShapeDtypeStruct((parts, piece, model), BF16),
        in_specs=[vmem] * 8 + [anywhere] * 5,
        out_specs=vmem,
        scratch_shapes=[
            pltpu.VMEM((ROWS, pool), F32),
            pltpu.VMEM((ROWS, own), F32),
            pltpu.VMEM((n, ROWS, feats), BF16),
            pltpu.VMEM((n, ROWS, feats), BF16),
            pltpu.VMEM((n, 8, ROWS), F32),
            pltpu.VMEM((n, 8, ROWS), F32),
            pltpu.VMEM((parts, n, chips, piece, cols), BF16),
            pltpu.VMEM((2, feats, width), BF16),
            pltpu.VMEM((2, width, hidden), BF16),
            pltpu.VMEM((2, width, hidden), BF16),
            pltpu.VMEM((2, hidden, width), BF16),
            pltpu.VMEM((parts, n, chips, piece, feats), BF16),
            pltpu.VMEM((parts, n, chips, piece, cols), BF16),
            pltpu.VMEM((parts, n, chips, piece, cols), BF16),
            pltpu.VMEM((parts, n, chips, piece, cols), BF16),
            pltpu.VMEM((parts, n, chips, piece, cols), F32),
            pltpu.VMEM((parts, n, chips, piece, cols), BF16),
            pltpu.VMEM((parts, 2, n, chips, piece, hidden), BF16),
            pltpu.VMEM((parts, chips, 2, n, piece, hidden), BF16),
            pltpu.VMEM((parts, n, chips, piece, HEAD), F32),
            pltpu.VMEM((parts, chips, n, piece, HEAD), F32),
            pltpu.VMEM((parts, n, chips, piece, hidden), BF16),
            pltpu.VMEM((parts, n, chips, piece, cols), BF16),
            pltpu.VMEM((parts, n, chips, piece, cols), BF16),
            pltpu.VMEM((parts, chips, piece, cols), BF16),
            pltpu.VMEM((parts, chips, piece, cols), BF16),
            pltpu.SemaphoreType.DMA((4,)),
            *dma(4),
            pltpu.SemaphoreType.DMA((parts,)),
            *dma(parts, chips),
            *dma(n),
            *dma(n),
            *dma(parts, chips),
            *dma(parts, n),
            *dma(parts, n),
            *dma(parts, chips, 2),
            *dma(parts, chips),
            *dma(parts, chips),
            *dma(parts, n),
            *dma(parts, chips),
        ],
        compiler_params=pltpu.CompilerParams(
            collective_id=0, has_side_effects=True, vmem_limit_bytes=60 * 1024 * 1024
        ),
    )(
        queries[0],
        kv_pages.reshape(pool, kv_pages.shape[3]),
        fresh_kv[0],
        norm_gain[None],
        page_table[0],
        shared_pages,
        cache_lens.reshape(DECODES, 1),
        prefill_offsets.reshape(1, 1),
        residual.reshape(n, parts, piece, model),
        out_weight,
        gate_weight,
        up_weight,
        down_weight,
    )
    return result.reshape(1, own, model)


def solution(mesh):
    placed = (
        P("grp", None, None),
        P("grp", "mlp", None),
        P("grp", "mlp", None, None),
        P("grp", None, None),
        P(),
        P("mlp", "grp"),
        P("grp", "mlp"),
        P("grp", "mlp"),
        P("mlp", "grp"),
        P("grp", None, None),
        P("grp", None),
        P("grp", None),
        P("grp"),
    )
    return jax.shard_map(
        functools.partial(local, mesh.shape["mlp"], mesh.shape["grp"] // 2),
        mesh=mesh,
        in_specs=placed,
        out_specs=P("grp", "mlp", None),
        check_vma=False,
    )
```

time: 597 us -> 166 us (0.28)
  waiting for transfers between devices: 434 us -> 0 us
  Pallas kernels: 0 us -> 160 us
  matrix products: 46 us -> 0 us
  other arithmetic: 36.5 us -> 0 us
  blocking collectives: 35.3 us -> 0 us
  local copies, waits for them, and re-layouts: 29.8 us -> 4.35 us
  between operations: 14.6 us -> 0.66 us
    all_gather x5 -> x0, waiting for transfers between devices: 354 us -> none  [the longest x1 111 us: merged(): everything = jax.tree.map(lambda part: lax.all_gather(part, axis), shard)]
    pallas_call x0 -> x1, Pallas kernels: none -> 160 us  [local(): pl.pallas_call(functools.partial(kernel, n, chips), out_shape=jax.ShapeDt...]
    psum x1 -> x0, waiting for transfers between devices: 49.9 us -> none  [local(): lax.psum(jnp.dot(own_features, out_rows, preferred_element_type=jnp.float...]
    dot_general x19 -> x0, matrix products: 46 us -> none  [the longest x1 12.9 us: local(): jnp.dot(hidden, down_rows, preferred_element_type=jnp.float32)]
    all_gather x2 -> x0, blocking collectives: 35.3 us -> none  [merged(): everything = jax.tree.map(lambda part: lax.all_gather(part, axis), shard)]
    reduce_scatter x1 -> x0, waiting for transfers between devices: 27.3 us -> none  [local(): lax.psum_scatter(jnp.dot(hidden, down_rows, preferred_element_type=jnp.fl...]
    add x15 -> x0, other arithmetic: 21 us -> none  [the longest x3 17.3 us: combine_parts(): mixed_one.reshape(row_number, head_number, -1) * factor_one[:, :, None]]
    reduce_sum x5 -> x0, other arithmetic: 9.77 us -> none  [the longest x2 6.96 us: local(): row_total = jnp.sum(cache_exps, axis=2) + jnp.sum(fresh_exps, axis=2)]
  transfers between devices with their start and end apart: 7 -> 0, of which waited for: 7 -> 0; matrix products, arithmetic and copies ran while one was open for 7% -> 0% of each run, Pallas kernels for 0% -> 0%
where the time goes in v1:
time: 166 us; the launch traced here: 165 us
  Pallas kernels  160 us (96%)
  local copies, waits for them, and re-layouts  4.35 us (3%)
    pallas_call x1, Pallas kernels, local(): pl.pallas_call(functools.partial(kernel, n, chips), out_shape=jax.ShapeDt...  160 us

profile of v1, /device:TPU:0, one launch (start us, length us, event | category | flops | bytes accessed | tf_op | source)
XLA Modules:
  0.0 165.4 jit_solution(15721753655012045007)
XLA Ops:
  0.7 1.4 copy.14
  2.0 1.3 copy.15.lens
  3.3 160.3 %shard_map.127 = bf16[2,16,4096]{2,1,0:T(8,128)(2,1)} custom-call(bf16[128,4096]{1,0:T(8,128)(2,1)} %bitcast.12, bf16[1024,1024]{1,0:T(8,128)(2,1)} %bitcast.10, bf16[32,1024]{1,0:T(8,128)(2,1)} %bitcast.14, f32[1,4096]{1,0:T(1,128)} %bitcast.16, s32[16,12]{1,0:T(8,128)} %bitcast.15, s32[1,4]{1,0:T(1,128)} %shared.1, s32[16,1]{1,0:T(8,128)} %copy.15.lens, ...), custom_call_target="tpu_custom_call" | custom-call | tf_op jit(solution)/shard_map/pallas_call | solution.py:524
  163.7 1.7 %copy.18 = bf16[1,32,4096]{2,1,0:T(8,128)(2,1)} copy(bf16[1,32,4096]{2,1,0:T(8,128)(2,1)} %bitcast.11) | data formatting | bytes 524288

commit v2 on v1

--- a/solution.py
+++ b/solution.py
@@ -185,118 +185,156 @@
     pool_pages = kv_pages.shape[0] // PAGE
     own_count = fresh_kv.shape[0]
     token = lax.broadcasted_iota(jnp.int32, (1, PAGE), 1)
-    slot_ids = lax.broadcasted_iota(jnp.int32, (DECODES, PRIVATE_PAGES), 1)
+    slot_ids = lax.broadcasted_iota(jnp.int32, (PRIVATE_PAGES, DECODES), 0)
     shared_ids = lax.broadcasted_iota(jnp.int32, (1, SHARED_PAGES), 1)
+    diagonal = lax.broadcasted_iota(jnp.int32, (DECODES, DECODES), 0) == (
+        lax.broadcasted_iota(jnp.int32, (DECODES, DECODES), 1)
+    )
+
+    def upright(row):
+        return jnp.sum(jnp.where(diagonal, row, 0), axis=1, keepdims=True)
+
+    limits = upright(lens[...])
     for p in range(pool_pages):
         page_id = me * pool_pages + p
         own = table[...] == page_id
-        own_any = jnp.max(jnp.where(own, 1, 0), axis=1, keepdims=True)
-        own_base = jnp.sum(
-            jnp.where(own, (SHARED_PAGES + slot_ids) * PAGE, 0), axis=1, keepdims=True
+        own_any = upright(jnp.max(jnp.where(own, 1, 0), axis=0, keepdims=True))
+        own_base = upright(
+            jnp.sum(
+                jnp.where(own, (SHARED_PAGES + slot_ids) * PAGE, 0), axis=0, keepdims=True
+            )
         )
         match = shared[...] == page_id
         is_shared = jnp.max(jnp.where(match, 1, 0), axis=1, keepdims=True)
         shared_base = jnp.sum(jnp.where(match, shared_ids * PAGE, 0), axis=1, keepdims=True)
         position = shared_base + token
-        seen = (is_shared > 0) & (position < offset[...])
-        bias[0:PREFILL, p * PAGE : (p + 1) * PAGE] = jnp.broadcast_to(
-            jnp.where(seen, 0.0, NEG_FILL), (PREFILL, PAGE)
-        )
+        seen = (is_shared > 0) & (position < offset[0])
+        prefill_bias = jnp.broadcast_to(jnp.where(seen, 0.0, NEG_FILL), (PREFILL, PAGE))
         belongs = jnp.maximum(own_any, is_shared)
         base = jnp.where(is_shared > 0, shared_base, own_base)
-        seen = (belongs > 0) & (base + token < lens[...])
-        bias[PREFILL:ROWS, p * PAGE : (p + 1) * PAGE] = jnp.where(seen, 0.0, NEG_FILL)
+        seen = (belongs > 0) & (base + token < limits)
+        decode_bias = jnp.where(seen, 0.0, NEG_FILL)
+        bias[:, :, :, p * PAGE : (p + 1) * PAGE] = jnp.concatenate(
+            [prefill_bias, decode_bias], axis=0
+        ).reshape(n, parts, piece, PAGE)
     row_ids = lax.broadcasted_iota(jnp.int32, (ROWS, own_count), 0)
     key_rows = me * own_count + lax.broadcasted_iota(jnp.int32, (ROWS, own_count), 1)
     seen = ((row_ids < PREFILL) & (key_rows < PREFILL) & (key_rows <= row_ids)) | (
         (row_ids >= PREFILL) & (key_rows == row_ids)
     )
-    fresh_bias[...] = jnp.where(seen, 0.0, NEG_FILL)
-
-    lane = lax.broadcasted_iota(jnp.int32, (ROWS, HEAD), 1)
+    fresh_bias[...] = jnp.where(seen, 0.0, NEG_FILL).reshape(n, parts, piece, own_count)
+
     scale = HEAD ** (-0.5)
     keys_across = (((1,), (1,)), ((), ()))
     value_at = KV_HEADS * HEAD
-
-    part_copies = []
-    stat_copies = []
-    for j in range(1, n + 1):
-        block = lax.rem(me + j, n)
-
-        def one_head(i, stats, block=block):
-            head = block * block_heads + i
-            key_start = pl.multiple_of((head // GROUPED) * HEAD, HEAD)
-            query = queries[:, pl.ds(pl.multiple_of(head * HEAD, HEAD), HEAD)]
-            scores = (
-                lax.dot_general(
-                    query,
-                    kv_pages[:, pl.ds(key_start, HEAD)],
-                    keys_across,
-                    preferred_element_type=F32,
-                )
-                * scale
-                + bias[...]
-            )
-            fresh_scores = (
-                lax.dot_general(
-                    query,
-                    fresh_kv[:, pl.ds(key_start, HEAD)],
-                    keys_across,
-                    preferred_element_type=F32,
-                )
-                * scale
-                + fresh_bias[...]
-            )
+    rows_here = n * piece
+    stacked = block_heads * rows_here
+    lane = lax.broadcasted_iota(jnp.int32, (rows_here, ROWS), 1)
+
+    def part_copy(q, j, block):
+        return pltpu.make_async_remote_copy(
+            src_ref=part_send.at[q, block],
+            dst_ref=part_recv.at[q, j],
+            send_sem=part_ss.at[q, j],
+            recv_sem=part_rs.at[q, j],
+            device_id=along(j),
+            device_id_type=MESH,
+        )
+
+    def stat_copy(q, j, block):
+        return pltpu.make_async_remote_copy(
+            src_ref=stat_send.at[q, block],
+            dst_ref=stat_recv.at[q, j],
+            send_sem=stat_ss.at[q, j],
+            recv_sem=stat_rs.at[q, j],
+            device_id=along(j),
+            device_id_type=MESH,
+        )
+
+    for q in range(parts):
+
+        @pl.loop(1, n + 1)
+        def _(j, q=q):
+            block = lax.rem(me + j, n)
+            key_start = pl.multiple_of((block * block_heads // GROUPED) * HEAD, HEAD)
+            query = jnp.concatenate(
+                [
+                    queries[
+                        :, q, :, pl.ds(pl.multiple_of((block * block_heads + i) * HEAD, HEAD), HEAD)
+                    ].reshape(rows_here, HEAD)
+                    for i in range(block_heads)
+                ],
+                axis=0,
+            )
+            here = bias[:, q].reshape(1, rows_here, pool_pages * PAGE)
+            fresh_here = fresh_bias[:, q].reshape(1, rows_here, own_count)
+            scores = lax.dot_general(
+                query,
+                kv_pages[:, pl.ds(key_start, HEAD)],
+                keys_across,
+                preferred_element_type=F32,
+            )
+            scores = scores.reshape(block_heads, rows_here, -1) * scale + here
+            fresh_scores = lax.dot_general(
+                query,
+                fresh_kv[:, pl.ds(key_start, HEAD)],
+                keys_across,
+                preferred_element_type=F32,
+            )
+            fresh_scores = fresh_scores.reshape(block_heads, rows_here, -1) * scale + fresh_here
             peak = jnp.maximum(
-                jnp.max(scores, axis=1, keepdims=True),
-                jnp.max(fresh_scores, axis=1, keepdims=True),
+                jnp.max(scores, axis=2, keepdims=True),
+                jnp.max(fresh_scores, axis=2, keepdims=True),
             )
             exps = jnp.exp(scores - peak)
             fresh_exps = jnp.exp(fresh_scores - peak)
-            total = jnp.sum(exps, axis=1, keepdims=True) + jnp.sum(
-                fresh_exps, axis=1, keepdims=True
+            total = jnp.sum(exps, axis=2, keepdims=True) + jnp.sum(
+                fresh_exps, axis=2, keepdims=True
             )
             mixed = jnp.dot(
-                exps.astype(BF16),
+                exps.astype(BF16).reshape(stacked, pool_pages * PAGE),
                 kv_pages[:, pl.ds(value_at + key_start, HEAD)],
                 preferred_element_type=F32,
             ) + jnp.dot(
-                fresh_exps.astype(BF16),
+                fresh_exps.astype(BF16).reshape(stacked, own_count),
                 fresh_kv[:, pl.ds(value_at + key_start, HEAD)],
                 preferred_element_type=F32,
             )
-            part_send[block, :, pl.ds(pl.multiple_of(i * HEAD, HEAD), HEAD)] = (
-                mixed / total
-            ).astype(BF16)
-            return jnp.where(lane == i, peak + jnp.log(total), stats)
-
-        stats = lax.fori_loop(0, block_heads, one_head, jnp.zeros((ROWS, HEAD), F32), unroll=2)
-        stat_send[block] = stats.T[0:8]
-        if j < n:
-            part_copies.append(
-                send(part_send.at[block], part_recv.at[j], part_ss.at[j], part_rs.at[j], along(j))
-            )
-            stat_copies.append(
-                send(stat_send.at[block], stat_recv.at[j], stat_ss.at[j], stat_rs.at[j], along(j))
-            )
-
-    for copy in stat_copies + part_copies:
-        copy.wait_recv()
-    levels = [stat_send[me].T] + [stat_recv[j].T for j in range(1, n)]
-    top = functools.reduce(jnp.maximum, levels)
-    shares = [jnp.exp(level - top) for level in levels]
-    whole = functools.reduce(jnp.add, shares)
-    shares = [share / whole for share in shares]
-    for i in range(block_heads):
-        span = slice(i * HEAD, (i + 1) * HEAD)
-        value = part_send[me, :, span].astype(F32) * shares[0][:, i : i + 1]
-        for j in range(1, n):
-            value = value + part_recv[j, :, span].astype(F32) * shares[j][:, i : i + 1]
-        value = value.astype(BF16).reshape(n, parts, piece, HEAD)
-        for q in range(parts):
-            att[q, :, 0, :, span] = value[:, q]
+            mixed = (mixed.reshape(block_heads, rows_here, HEAD) / total).astype(BF16)
+            level = peak + jnp.log(total)
+            stats = jnp.zeros((rows_here, ROWS), F32)
+            for i in range(block_heads):
+                part_send[q, block, :, i * HEAD : (i + 1) * HEAD] = mixed[i]
+                stats = jnp.where(lane == i, level[i], stats)
+            if rows_here < ROWS:
+                stats = jnp.concatenate(
+                    [stats, jnp.zeros((ROWS - rows_here, ROWS), F32)], axis=0
+                )
+            stat_send[q, block] = stats.T[0:8]
+
+            @pl.when(j < n)
+            def _():
+                part_copy(q, j, block).start()
+                stat_copy(q, j, block).start()
+
     att_copies = [[] for _ in range(parts)]
     for q in range(parts):
+        for j in range(1, n):
+            stat_copy(q, j, lax.rem(me + j, n)).wait_recv()
+            part_copy(q, j, lax.rem(me + j, n)).wait_recv()
+        levels = [stat_send[q, me].T] + [stat_recv[q, j].T for j in range(1, n)]
+        top = functools.reduce(jnp.maximum, levels)
+        shares = [jnp.exp(level - top) for level in levels]
+        whole = functools.reduce(jnp.add, shares)
+        shares = [share / whole for share in shares]
+        for i in range(block_heads):
+            span = slice(i * HEAD, (i + 1) * HEAD)
+            value = part_send[q, me, :, span].astype(F32) * shares[0][0:rows_here, i : i + 1]
+            for j in range(1, n):
+                value = value + (
+                    part_recv[q, j, :, span].astype(F32) * shares[j][0:rows_here, i : i + 1]
+                )
+            att[q, :, 0, :, span] = value.astype(BF16).reshape(n, piece, HEAD)
         for j in range(1, chips):
             att_copies[q].append(
                 send(att.at[q, :, 0], att.at[q, :, j], att_ss.at[q, j], att_rs.at[q, j], across(j))
@@ -481,7 +519,11 @@
             start = pl.multiple_of(lax.rem(chip + j, chips) * cols, cols)
             out[q, :, pl.ds(start, cols)] = fin_recv[q, j]
 
-    sent = paired + res_copies + part_copies + stat_copies
+    sent = paired + res_copies
+    for q in range(parts):
+        for j in range(1, n):
+            sent.append(part_copy(q, j, lax.rem(me + j, n)))
+            sent.append(stat_copy(q, j, lax.rem(me + j, n)))
     for group in (att_copies, rs_copies, ag_copies, gu_copies, hid_copies, down_copies, fin_copies):
         for copies in group:
             sent = sent + copies
@@ -524,15 +566,15 @@
     result = pl.pallas_call(
         functools.partial(kernel, n, chips),
         out_shape=jax.ShapeDtypeStruct((parts, piece, model), BF16),
-        in_specs=[vmem] * 8 + [anywhere] * 5,
+        in_specs=[vmem] * 7 + [pl.BlockSpec(memory_space=pltpu.SMEM)] + [anywhere] * 5,
         out_specs=vmem,
         scratch_shapes=[
-            pltpu.VMEM((ROWS, pool), F32),
-            pltpu.VMEM((ROWS, own), F32),
-            pltpu.VMEM((n, ROWS, feats), BF16),
-            pltpu.VMEM((n, ROWS, feats), BF16),
-            pltpu.VMEM((n, 8, ROWS), F32),
-            pltpu.VMEM((n, 8, ROWS), F32),
+            pltpu.VMEM((n, parts, piece, pool), F32),
+            pltpu.VMEM((n, parts, piece, own), F32),
+            pltpu.VMEM((parts, n, n * piece, feats), BF16),
+            pltpu.VMEM((parts, n, n * piece, feats), BF16),
+            pltpu.VMEM((parts, n, 8, ROWS), F32),
+            pltpu.VMEM((parts, n, 8, ROWS), F32),
             pltpu.VMEM((parts, n, chips, piece, cols), BF16),
             pltpu.VMEM((2, feats, width), BF16),
             pltpu.VMEM((2, width, hidden), BF16),
@@ -557,8 +599,8 @@
             *dma(4),
             pltpu.SemaphoreType.DMA((parts,)),
             *dma(parts, chips),
-            *dma(n),
-            *dma(n),
+            *dma(parts, n),
+            *dma(parts, n),
             *dma(parts, chips),
             *dma(parts, n),
             *dma(parts, n),
@@ -572,14 +614,14 @@
             collective_id=0, has_side_effects=True, vmem_limit_bytes=60 * 1024 * 1024
         ),
     )(
-        queries[0],
+        queries.reshape(n, parts, piece, queries.shape[2]),
         kv_pages.reshape(pool, kv_pages.shape[3]),
         fresh_kv[0],
         norm_gain[None],
-        page_table[0],
+        page_table[0].T,
         shared_pages,
-        cache_lens.reshape(DECODES, 1),
-        prefill_offsets.reshape(1, 1),
+        cache_lens,
+        prefill_offsets,
         residual.reshape(n, parts, piece, model),
         out_weight,
         gate_weight,

time: 166 us -> 157 us (0.946)
  Pallas kernels: 160 us -> 153 us
    pallas_call x1, Pallas kernels: 160 us -> 153 us  [local(): pl.pallas_call(functools.partial(kernel, n, chips), out_shape=jax.ShapeDt...]
where the time goes in v2:
time: 157 us
  Pallas kernels  153 us (97%)
  local copies, waits for them, and re-layouts  2.96 us (2%)
    pallas_call x1, Pallas kernels, local(): pl.pallas_call(functools.partial(kernel, n, chips), out_shape=jax.ShapeDt...  153 us

profile of v2, /device:TPU:0, one launch (start us, length us, event | category | flops | bytes accessed | tf_op | source)
XLA Modules:
  0.0 157.0 jit_solution(5769733071301574398)
XLA Ops:
  0.7 1.3 copy.16
  1.9 153.4 %shard_map.127 = bf16[2,16,4096]{2,1,0:T(8,128)(2,1)} custom-call(bf16[4,2,16,4096]{3,2,1,0:T(8,128)(2,1)} %bitcast.12, bf16[1024,1024]{1,0:T(8,128)(2,1)} %bitcast.11, bf16[32,1024]{1,0:T(8,128)(2,1)} %bitcast.15, f32[1,4096]{1,0:T(1,128)} %bitcast.17, s32[12,16]{1,0:T(8,128)} %bitcast.16, s32[1,4]{1,0:T(1,128)} %shared.1, s32[1,16]{1,0:T(1,128)} %lens.1, ...), custom_call_target="tpu_custom_call" | custom-call | tf_op jit(solution)/shard_map/pallas_call | solution.py:566
  155.4 1.7 %copy.19 = bf16[1,32,4096]{2,1,0:T(8,128)(2,1)} copy(bf16[1,32,4096]{2,1,0:T(8,128)(2,1)} %bitcast.14) | data formatting | bytes 524288

commit v3 on v2

--- a/solution.py
+++ b/solution.py
@@ -549,7 +549,7 @@
     prefill_offsets,
 ):
     own = fresh_kv.shape[1]
-    parts = max(1, own // 16)
+    parts = max(1, own // 8)
     piece = own // parts
     width = out_weight.shape[1]
     cols = 2 * width

time: 157 us -> 153 us (0.975)
  Pallas kernels: 153 us -> 149 us
    pallas_call x1, Pallas kernels: 153 us -> 149 us  [local(): pl.pallas_call(functools.partial(kernel, n, chips), out_shape=jax.ShapeDt...]
where the time goes in v3:
time: 153 us
  Pallas kernels  149 us (97%)
  local copies, waits for them, and re-layouts  2.96 us (2%)
    pallas_call x1, Pallas kernels, local(): pl.pallas_call(functools.partial(kernel, n, chips), out_shape=jax.ShapeDt...  149 us

profile of v3, /device:TPU:0, one launch (start us, length us, event | category | flops | bytes accessed | tf_op | source)
XLA Modules:
  0.0 152.8 jit_solution(13215132113390085440)
XLA Ops:
  0.7 1.3 copy.16
  1.9 149.2 %shard_map.127 = bf16[4,8,4096]{2,1,0:T(8,128)(2,1)} custom-call(bf16[4,4,8,4096]{3,2,1,0:T(8,128)(2,1)} %bitcast.12, bf16[1024,1024]{1,0:T(8,128)(2,1)} %bitcast.11, bf16[32,1024]{1,0:T(8,128)(2,1)} %bitcast.15, f32[1,4096]{1,0:T(1,128)} %bitcast.17, s32[12,16]{1,0:T(8,128)} %bitcast.16, s32[1,4]{1,0:T(1,128)} %shared.1, s32[1,16]{1,0:T(1,128)} %lens.1, ...), custom_call_target="tpu_custom_call" | custom-call | tf_op jit(solution)/shard_map/pallas_call | solution.py:566
  151.2 1.7 %copy.19 = bf16[1,32,4096]{2,1,0:T(8,128)(2,1)} copy(bf16[1,32,4096]{2,1,0:T(8,128)(2,1)} %bitcast.14) | data formatting | bytes 524288
